TPU v7x, 32 devices: a whole 2x2x4 slice. The times are simulated.
32 devices in a mesh: ctx: 2 (over y), exp: 16 (over z, x, core).
Axes of the slice: x: 2, y: 2, z: 4, core: 2. Of those that a mesh axis runs over, the one named last changes fastest.
Arguments:
- hidden_in: bfloat16 [16, 256, 2048], P('exp', 'ctx'), may hold values from -3 to 3
- query: bfloat16 [16, 256, 4096], P('exp', 'ctx'), may hold values from -96 to 96
- keyval: bfloat16 [16, 256, 512], P('exp', 'ctx'), may hold values from -5 to 5
- out_proj: bfloat16 [4096, 2048], P('exp'), may hold values from -0.375 to 0.375
- norm_gain: bfloat16 [2048], replicated, may hold values from 0.099609375 to 1.8984375
- expert_ids: int32 [16, 256, 8], P('exp', 'ctx'), may hold values from 0 to 15, all different within a row; in each aligned block of 128 rows (0 to 127, 128 to 255, ..., all dimensions but the last counted through in order) at most 68 rows name the same one
- gate_weights: float32 [16, 256, 8], P('exp', 'ctx'), may hold values from 0.1 to 0.4
- w_gate: bfloat16 [16, 2048, 768], P('exp'), may hold values from -0.125 to 0.125
- w_up: bfloat16 [16, 2048, 768], P('exp'), may hold values from -0.125 to 0.125
- w_down: bfloat16 [16, 768, 2048], P('exp'), may hold values from -0.21875 to 0.21875
Outputs:
- layer_out: bfloat16 [16, 256, 2048], P('exp', 'ctx')
Inputs may be any that keep to these rules, and one draw needn't show every extreme that they name: `expert_ids`: in each aligned block of 128 tokens (the tokens of one device) no expert is named by more than 68 tokens, a bound that some block reaches; a token names 8 different experts.
All inputs are finite; a program needn't handle non-finite values.
Results may differ from a plain program's by a relative error of at most 0.014.
Values may be sent and summed in bfloat16 or wider, within the bound.
No kernel may reach another device: no remote copies, remote signals or barrier semaphores. Data moves between devices by JAX's collectives and lax.ppermute only.
A program may use at most 128 MiB of HBM per device.

v0:
```python
import functools

import jax
import jax.numpy as jnp
from jax import lax
from jax.experimental import pallas as pl
from jax.experimental.pallas import tpu as pltpu
from jax.sharding import PartitionSpec as P

D = 2048
QH = 32
KVH = 2
HD = 128
TOP = 8
LANES = 128
TERMS = 3
TILE = 512
GROUP = 256


def chip_ring(n):
    chips = n // 2
    return list(range(0, chips, 2)) + list(range(1, chips, 2))[::-1]


def device_ring(n):
    return [2 * chip + core for chip in chip_ring(n) for core in range(2)]


def rotate(block, axis, distance):
    n = lax.axis_size(axis)
    return lax.ppermute(block, axis, [(i, (i + distance) % n) for i in range(n)])


def attention_kernel(places, pos_ref, query_ref, *refs):
    *kv_refs, out_ref = refs
    n_ctx = len(kv_refs)
    position = pos_ref[0]
    rows = query_ref.shape[0]
    row = lax.broadcasted_iota(jnp.int32, (rows, rows), 0)
    col = lax.broadcasted_iota(jnp.int32, (rows, rows), 1)
    visible = [row >= col]
    for back in range(1, n_ctx):
        visible.append(jnp.full((rows, rows), position, jnp.int32) >= back)
    visible = jnp.concatenate(visible, axis=1)
    for kv_head in range(KVH):
        k_at = kv_head * HD
        v_at = (KVH + kv_head) * HD
        keys = jnp.concatenate([ref[:, k_at : k_at + HD] for ref in kv_refs], axis=0)
        values = jnp.concatenate([ref[:, v_at : v_at + HD] for ref in kv_refs], axis=0)
        for group in range(QH // KVH):
            head = kv_head * (QH // KVH) + group
            scores = lax.dot_general(
                query_ref[:, head * HD : (head + 1) * HD],
                keys,
                (((1,), (1,)), ((), ())),
                preferred_element_type=jnp.float32,
            ) * HD ** (-0.5)
            scores = jnp.where(visible, scores, -1e30)
            weights = jnp.exp(scores - jnp.max(scores, axis=1, keepdims=True))
            row_sum = jnp.sum(weights, axis=1, keepdims=True)
            mixed = jnp.dot(
                weights.astype(jnp.bfloat16), values, preferred_element_type=jnp.float32
            )
            at = places[head]
            out_ref[:, at : at + HD] = (mixed / row_sum).astype(jnp.bfloat16)


def norm_kernel(experts_all, pos_ref, hidden_ref, *refs):
    *projected_refs, gain_ref, ids_ref, gates_ref, residual_ref, tokens_ref = refs
    n_ctx = len(projected_refs)
    wide = D // n_ctx
    square_sum = None
    for back, ref in enumerate(projected_refs):
        at = pl.ds(pl.multiple_of(lax.rem(pos_ref[0] + back, n_ctx) * wide, wide), wide)
        part = hidden_ref[:, at].astype(jnp.float32) + ref[...].astype(jnp.float32)
        residual_ref[:, at] = part
        squares = jnp.sum(part * part, axis=1, keepdims=True)
        square_sum = squares if square_sum is None else square_sum + squares
    scale_inv = lax.rsqrt(square_sum * (1.0 / D) + 1e-06)
    normed = residual_ref[...] * scale_inv * gain_ref[...].astype(jnp.float32)
    tokens_ref[:, :D] = normed.astype(jnp.bfloat16)
    shape = (tokens_ref.shape[0], tokens_ref.shape[1] - D)
    column = lax.broadcasted_iota(jnp.int32, shape, 1)
    expert = lax.rem(column, experts_all)
    gates = jnp.zeros(shape, jnp.float32)
    for k in range(TOP):
        gates = gates + jnp.where(ids_ref[:, k : k + 1] == expert, gates_ref[:, k : k + 1], 0.0)
    terms = jnp.zeros(shape, jnp.float32)
    for term in range(TERMS):
        rounded = gates.astype(jnp.bfloat16).astype(jnp.float32)
        terms = jnp.where(column // experts_all == term, rounded, terms)
        gates = gates - rounded
    tokens_ref[:, D:] = terms.astype(jnp.bfloat16)


def expert_kernel(
    experts_all, slots, expert_ref, tokens_ref, gate_ref, up_ref, down_ref, out_ref, picked_ref
):
    groups = tokens_ref.shape[0] // GROUP
    row = lax.broadcasted_iota(jnp.int32, (GROUP, GROUP), 0)
    col = lax.broadcasted_iota(jnp.int32, (GROUP, GROUP), 1)
    up_to = (row >= col).astype(jnp.bfloat16)
    slot_row = lax.broadcasted_iota(jnp.int32, (slots, GROUP), 0).astype(jnp.float32)
    slot_col = lax.broadcasted_iota(jnp.int32, (GROUP, slots), 1).astype(jnp.float32)
    weights, places = [], []
    for g in range(groups):
        at = pl.ds(g * GROUP, GROUP)
        terms = tokens_ref[at, D:].astype(jnp.float32)
        column = lax.broadcasted_iota(jnp.int32, terms.shape, 1)
        mine = (lax.rem(column, experts_all) == expert_ref[0]) & (column < TERMS * experts_all)
        gates = jnp.sum(jnp.where(mine, terms, 0.0), axis=1, keepdims=True)
        named = jnp.broadcast_to(gates > 0.0, (GROUP, LANES))
        rank = jnp.dot(
            up_to, named.astype(jnp.bfloat16), preferred_element_type=jnp.float32
        )
        place = jnp.where(named, rank - 1.0, -1.0)
        pick = (slot_row == jnp.transpose(place)[:1]).astype(jnp.bfloat16)
        picked = jnp.dot(pick, tokens_ref[at, :D], preferred_element_type=jnp.float32)
        picked_ref[pl.ds(g * slots, slots), :] = picked.astype(jnp.bfloat16)
        weights.append(gates)
        places.append(place[:, :1])
    picked = picked_ref[...]
    gate_pre = jnp.dot(picked, gate_ref[...], preferred_element_type=jnp.float32)
    up_pre = jnp.dot(picked, up_ref[...], preferred_element_type=jnp.float32)
    activated = (gate_pre / (1.0 + jnp.exp(-gate_pre)) * up_pre).astype(jnp.bfloat16)
    picked_ref[...] = jnp.dot(
        activated, down_ref[...], preferred_element_type=jnp.float32
    ).astype(jnp.bfloat16)
    for g in range(groups):
        put = (slot_col == places[g]).astype(jnp.bfloat16)
        expert_out = jnp.dot(
            put, picked_ref[pl.ds(g * slots, slots), :], preferred_element_type=jnp.float32
        )
        out_ref[pl.ds(g * GROUP, GROUP), :] = (expert_out * weights[g]).astype(jnp.bfloat16)


def vmem():
    return pl.BlockSpec(memory_space=pltpu.VMEM)


def smem():
    return pl.BlockSpec(memory_space=pltpu.SMEM)


def attend(position, queries, blocks, n_exp, proj_rows):
    ring = device_ring(n_exp)
    places = {}
    for head in range(QH):
        device, inside = divmod(head * HD, proj_rows)
        places[head] = ring.index(device) * proj_rows + inside
    return pl.pallas_call(
        functools.partial(attention_kernel, places),
        out_shape=jax.ShapeDtypeStruct(queries.shape, jnp.bfloat16),
        in_specs=[smem()] + [vmem()] * (1 + len(blocks)),
        out_specs=vmem(),
        compiler_params=pltpu.CompilerParams(vmem_limit_bytes=16 * 1024 * 1024),
        name="attention",
    )(position.reshape(1), queries, *blocks)


def run_expert(experts_all, block_rows, expert, tokens, w_gate, w_up, w_down):
    total, width = tokens.shape
    ef = w_gate.shape[1]
    share = block_rows * TOP // experts_all
    capacity = min(block_rows, share + block_rows * TOP // (16 * experts_all))
    slots = min(GROUP, -(-(GROUP // block_rows * capacity) // 16) * 16)
    held = pl.Buffered(1)
    return pl.pallas_call(
        functools.partial(expert_kernel, experts_all, slots),
        grid=(total // TILE,),
        out_shape=jax.ShapeDtypeStruct((total, D), jnp.bfloat16),
        in_specs=[
            smem(),
            pl.BlockSpec((TILE, width), lambda i: (i, 0)),
            pl.BlockSpec((D, ef), lambda i: (0, 0), pipeline_mode=held),
            pl.BlockSpec((D, ef), lambda i: (0, 0), pipeline_mode=held),
            pl.BlockSpec((ef, D), lambda i: (0, 0), pipeline_mode=held),
        ],
        out_specs=pl.BlockSpec((TILE, D), lambda i: (i, 0)),
        scratch_shapes=[pltpu.VMEM((TILE // GROUP * slots, D), jnp.bfloat16)],
        compiler_params=pltpu.CompilerParams(vmem_limit_bytes=36 * 1024 * 1024),
        cost_estimate=pl.CostEstimate(
            flops=4 * total * D * ef, bytes_accessed=4 * total * D + 6 * D * ef, transcendentals=0
        ),
        name="experts",
    )(expert.reshape(1), tokens, w_gate, w_up, w_down)


def body(
    hidden_in, query, keyval, out_proj, norm_gain, expert_ids, gate_weights, w_gate, w_up, w_down
):
    n_ctx = lax.axis_size("ctx")
    n_exp = lax.axis_size("exp")
    position = lax.axis_index("ctx")
    rows = hidden_in.shape[1]
    proj_rows = out_proj.shape[0]
    ring = [device_ring(n_exp)]

    wide = D // n_ctx
    columns = lax.dynamic_slice_in_dim(out_proj, position * wide, wide, axis=1)
    columns = lax.all_gather(columns, "exp", axis=0, tiled=True, axis_index_groups=ring)

    blocks = [keyval[0]] + [rotate(keyval[0], "ctx", back) for back in range(1, n_ctx)]
    attended = attend(position, query[0], blocks, n_exp, proj_rows)
    others = [rotate(attended, "ctx", back) for back in range(1, n_ctx)]
    projected = []
    for back in range(1, n_ctx):
        part = jnp.dot(others[back - 1], columns, preferred_element_type=jnp.float32)
        projected.append(rotate(part.astype(jnp.bfloat16), "ctx", -back))
    projected = [jnp.dot(attended, columns, preferred_element_type=jnp.float32)] + projected

    local_experts = w_gate.shape[0]
    experts_all = n_exp * local_experts
    extra = -(-TERMS * experts_all // LANES) * LANES
    residual, tokens = pl.pallas_call(
        functools.partial(norm_kernel, experts_all),
        out_shape=(
            jax.ShapeDtypeStruct((rows, D), jnp.float32),
            jax.ShapeDtypeStruct((rows, D + extra), jnp.bfloat16),
        ),
        in_specs=[smem()] + [vmem()] * (4 + n_ctx),
        out_specs=(vmem(), vmem()),
        compiler_params=pltpu.CompilerParams(vmem_limit_bytes=16 * 1024 * 1024),
        name="norm",
    )(
        position.reshape(1),
        hidden_in[0],
        *projected,
        norm_gain.reshape(1, D),
        expert_ids[0],
        gate_weights[0],
    )

    tokens_all = lax.all_gather(tokens, "exp", axis=0, tiled=True, axis_index_groups=ring)
    partial = None
    for local in range(local_experts):
        expert = lax.axis_index("exp") * local_experts + local
        weighted = run_expert(
            experts_all, rows, expert, tokens_all, w_gate[local], w_up[local], w_down[local]
        )
        partial = weighted if partial is None else partial + weighted
    expert_sum = lax.psum_scatter(
        partial, "exp", scatter_dimension=0, axis_index_groups=ring, tiled=True
    )
    result = (residual + expert_sum.astype(jnp.float32)).astype(jnp.bfloat16)
    return result[None]


def solution(mesh):
    in_specs = (
        P("exp", "ctx", None),
        P("exp", "ctx", None),
        P("exp", "ctx", None),
        P("exp", None),
        P(),
        P("exp", "ctx", None),
        P("exp", "ctx", None),
        P("exp", None, None),
        P("exp", None, None),
        P("exp", None, None),
    )
    out_specs = P("exp", "ctx", None)
    return jax.shard_map(body, mesh=mesh, in_specs=in_specs, out_specs=out_specs, check_vma=False)
```

profile of v0, /device:TPU:0, one launch (start us, length us, event | category | flops | bytes accessed | tf_op | source)
XLA Modules:
  0.0 222.1 jit_solution(18092136128471872555)
XLA Ops:
  6.5 0.0 copy-start
  6.5 0.0 all-gather.3.cloned.1.call-start
  6.5 1.2 copy-done
  7.8 0.8 constant_dynamic-slice_fusion
  8.6 0.0 all-gather.3.cloned.1.call-update
  8.6 0.0 all-gather.5.cloned.1.call-start
  8.7 3.0 %collective-permute-start = (bf16[128,512]{1,0:T(8,128)(2,1)}, bf16[128,512]{1,0:T(8,128)(2,1)S(1)}, u32[]{:S(2)}, u32[]{:S(2)}) collective-permute-start(bf16[128,512]{1,0:T(8,128)(2,1)} %bitcast.20), channel_id=1, source_target_pairs={{0,16},{16,0},{1,17},{17,1},{2,18},{18,2},{3,19},{19,3},{4,20},{20... | collective-permute-start | bytes 393224 | tf_op jit(solution)/shard_map/ppermute | solution.py:32
  11.7 3.7 %collective-permute-done.refs_1_ = bf16[128,512]{1,0:T(8,128)(2,1)S(1)} collective-permute-done((bf16[128,512]{1,0:T(8,128)(2,1)}, bf16[128,512]{1,0:T(8,128)(2,1)S(1)}, u32[]{:S(2)}, u32[]{:S(2)}) %collective-permute-start) | collective-permute-done | bytes 131104 | tf_op jit(solution)/shard_map/ppermute | solution.py:32
  15.4 0.0 copy-start.2
  15.4 1.2 copy-done.2
  16.6 0.0 copy-start.4
  16.6 0.9 copy-done.4
  17.5 2.0 attention.1
  19.5 1.8 collective-permute-start.1
  21.3 0.7 reshape.11.refs_2_
  22.0 0.8 copy.11
  22.8 0.8 copy.12
  23.6 20.3 %collective-permute-done.1 = bf16[128,4096]{1,0:T(8,128)(2,1)S(1)} collective-permute-done((bf16[128,4096]{1,0:T(8,128)(2,1)S(1)}, bf16[128,4096]{1,0:T(8,128)(2,1)S(1)}, u32[]{:S(2)}, u32[]{:S(2)}) %collective-permute-start.1) | collective-permute-done | bytes 1048608 | tf_op jit(solution)/shard_map/ppermute | solution.py:32
  44.0 17.3 %all-gather.3.cloned.1.call-done = bf16[4096,1024]{1,0:T(8,128)(2,1)} async-done(((bf16[256,1024]{1,0:T(8,128)(2,1)}), bf16[4096,1024]{1,0:T(8,128)(2,1)}) %all-gather.3.cloned.1.call-update) | async-done | bytes 8388624 | tf_op jit(solution)/shard_map/all_gather | solution.py:202
  61.3 0.0 copy-start.8
  61.3 4.9 %convolution_convert_fusion = bf16[128,1024]{1,0:T(8,128)(2,1)S(1)} fusion(bf16[128,4096]{1,0:T(8,128)(2,1)S(1)} %collective-permute-done.1, bf16[4096,1024]{1,0:T(8,128)(2,1)} %all-gather.3.cloned.1.call-done), kind=kOutput, calls=%fused_computation | convolution fusion | flops 1073872896 | bytes 9699328 | tf_op jit(solution)/shard_map/dot_general | solution.py:209
  66.1 0.0 copy-start.3
  66.2 1.5 collective-permute-start.2
  67.7 0.0 copy-done.8
  67.7 1.3 fusion.1.refs_0_
  69.0 5.6 %collective-permute-done.2.refs_1_ = bf16[128,1024]{1,0:T(8,128)(2,1)S(1)} collective-permute-done((bf16[128,1024]{1,0:T(8,128)(2,1)S(1)}, bf16[128,1024]{1,0:T(8,128)(2,1)S(1)}, u32[]{:S(2)}, u32[]{:S(2)}) %collective-permute-start.2) | collective-permute-done | bytes 262176 | tf_op jit(solution)/shard_map/ppermute | solution.py:32
  74.7 0.0 copy-done.3
  74.7 1.4 norm.1
  76.1 0.0 all-gather.5.cloned.1.call-update
  76.1 0.0 reduce-scatter.2.cloned.1.call-start
  76.2 52.1 %all-gather.5.cloned.1.call-done.tokens_ref = bf16[2048,2176]{1,0:T(8,128)(2,1)} async-done(((bf16[128,2176]{1,0:T(8,128)(2,1)}), bf16[2048,2176]{1,0:T(8,128)(2,1)}) %all-gather.5.cloned.1.call-update) | async-done | bytes 8912912 | tf_op jit(solution)/shard_map/all_gather | solution.py:235
  128.3 0.0 copy-start.5
  128.3 1.9 copy-done.5
  130.2 0.0 copy-start.6
  130.2 1.9 copy-done.6
  132.1 0.0 copy-start.7
  132.1 1.9 copy-done.7
  134.0 19.0 %experts.1 = bf16[2048,2048]{1,0:T(8,128)(2,1)S(1)} custom-call(s32[1]{0:T(128)} %bitcast.6.expert_ref, bf16[2048,2176]{1,0:T(8,128)(2,1)} %all-gather.5.cloned.1.call-done.tokens_ref, bf16[2048,768]{1,0:T(8,128)(2,1)S(1)} %bitcast.22, bf16[2048,768]{1,0:T(8,128)(2,1)S(1)} %bitcast.23, bf16[768,2048]{1,0:T(8,128)(2,1)S(1)} %bitcast.24), custom_call_target="tpu_custom_call" | custom-call | flops 12884901888 | bytes 26214400 | tf_op jit(solution)/shard_map/experts/pallas_call | solution.py:169
  152.9 0.0 copy-start.1
  152.9 3.2 %copy-done.1 = bf16[2048,2048]{1,0:T(8,128)(2,1)} copy-done((bf16[2048,2048]{1,0:T(8,128)(2,1)}, bf16[2048,2048]{1,0:T(8,128)(2,1)S(1)}, u32[]{:S(2)}) %copy-start.1) | copy-done | bytes 8388632
  156.2 0.0 reduce-scatter.2.cloned.1.call-update
  156.2 57.4 %reduce-scatter.2.cloned.1.call-done = bf16[128,2048]{1,0:T(8,128)(2,1)} async-done(((bf16[2048,2048]{1,0:T(8,128)(2,1)}), bf16[128,2048]{1,0:T(8,128)(2,1)}) %reduce-scatter.2.cloned.1.call-update) | async-done | bytes 524304 | tf_op jit(solution)/shard_map/reduce_scatter | solution.py:243
  213.6 1.9 fusion
Async XLA Ops:
  6.5 1.2 copy-start
  6.5 54.7 %all-gather.3.cloned.1.call-start = ((), (), s32[]{:S(2)}) async-start(), calls=%async_computation.1 | async-start | bytes 8912896 | tf_op jit(solution)/shard_map/all_gather | solution.py:202
  8.6 119.7 %all-gather.5.cloned.1.call-start = ((), (), s32[]{:S(2)}) async-start(), calls=%async_computation.2 | async-start | bytes 9469952 | tf_op jit(solution)/shard_map/all_gather | solution.py:235
  8.7 6.7 %collective-permute-start = (bf16[128,512]{1,0:T(8,128)(2,1)}, bf16[128,512]{1,0:T(8,128)(2,1)S(1)}, u32[]{:S(2)}, u32[]{:S(2)}) collective-permute-start(bf16[128,512]{1,0:T(8,128)(2,1)} %bitcast.20), channel_id=1, source_target_pairs={{0,16},{16,0},{1,17},{17,1},{2,18},{18,2},{3,19},{19,3},{4,20},{20... | collective-permute-start | bytes 393224 | tf_op jit(solution)/shard_map/ppermute | solution.py:32
  15.4 1.2 copy-start.2
  16.6 0.9 copy-start.4
  19.5 24.4 %collective-permute-start.1 = (bf16[128,4096]{1,0:T(8,128)(2,1)S(1)}, bf16[128,4096]{1,0:T(8,128)(2,1)S(1)}, u32[]{:S(2)}, u32[]{:S(2)}) collective-permute-start(bf16[128,4096]{1,0:T(8,128)(2,1)S(1)} %attention.1), channel_id=1, source_target_pairs={{0,16},{16,0},{1,17},{17,1},{2,18},{18,2},{3,19},{19,3},{4,20},{20... | collective-permute-start | bytes 3145736 | tf_op jit(solution)/shard_map/ppermute | solution.py:32
  61.3 6.4 %copy-start.8 = (bf16[4096,1024]{1,0:T(8,128)(2,1)S(1)}, bf16[4096,1024]{1,0:T(8,128)(2,1)}, u32[]{:S(2)}) copy-start(bf16[4096,1024]{1,0:T(8,128)(2,1)} %all-gather.3.cloned.1.call-done) | copy-start | bytes 25165828
  66.1 8.5 %copy-start.3 = (bf16[1,128,2048]{2,1,0:T(8,128)(2,1)S(1)}, bf16[1,128,2048]{2,1,0:T(8,128)(2,1)}, u32[]{:S(2)}) copy-start(bf16[1,128,2048]{2,1,0:T(8,128)(2,1)} %param.10) | copy-start | bytes 1572868
  66.2 8.5 %collective-permute-start.2 = (bf16[128,1024]{1,0:T(8,128)(2,1)S(1)}, bf16[128,1024]{1,0:T(8,128)(2,1)S(1)}, u32[]{:S(2)}, u32[]{:S(2)}) collective-permute-start(bf16[128,1024]{1,0:T(8,128)(2,1)S(1)} %convolution_convert_fusion), channel_id=1, source_target_pairs={{0,16},{16,0},{1,17},{17,1},{2,18},{18,2},{3,19},{19,3},{4,20},{20... | collective-permute-start | bytes 786440 | tf_op jit(solution)/shard_map/ppermute | solution.py:32
  76.1 137.5 %reduce-scatter.2.cloned.1.call-start = ((), (), s32[]{:S(2)}) async-start(), calls=%async_computation.3 | async-start | bytes 8912896 | tf_op jit(solution)/shard_map/reduce_scatter | solution.py:243
  128.3 1.9 copy-start.5
  130.2 1.9 copy-start.6
  132.1 1.9 copy-start.7
  152.9 3.2 %copy-start.1 = (bf16[2048,2048]{1,0:T(8,128)(2,1)}, bf16[2048,2048]{1,0:T(8,128)(2,1)S(1)}, u32[]{:S(2)}) copy-start(bf16[2048,2048]{1,0:T(8,128)(2,1)S(1)} %experts.1) | copy-start | bytes 25165828
Sparse Core Ops, SparseCore 0:
  9.0 52.2 all-gather.2
  76.2 52.0 all-gather.4
  156.3 57.2 reduce-scatter.1
where the time goes:
time: 223 us; the launch traced here: 222 us
  waiting for transfers between devices  157 us (70%)
  Pallas kernels  22.3 us (10%)
  local copies, waits for them, and re-layouts  15.4 us (7%)
  between operations  13.2 us (6%)
  starting transfers between devices  6.46 us (3%)
  matrix products  6.19 us (3%)
    reduce_scatter x1, waiting for transfers between devices, body(): lax.psum_scatter(partial, 'exp', scatter_dimension=0, axis_index_groups=r...  57.4 us
    all_gather x1, waiting for transfers between devices, body(): lax.all_gather(tokens, 'exp', axis=0, tiled=True, axis_index_groups=ring)  52.1 us
    ppermute x3, waiting for transfers between devices, rotate(): lax.ppermute(block, axis, [(i, (i + distance) % n) for i in range(n)])  29.7 us
    pallas_call x1, Pallas kernels, run_expert(): pl.pallas_call(functools.partial(expert_kernel, experts_all, slots), grid...  19 us
    all_gather x1, waiting for transfers between devices, body(): lax.all_gather(columns, 'exp', axis=0, tiled=True, axis_index_groups=ring)  17.3 us
    unnamed x20, local copies, waits for them, and re-layouts  13.8 us
    ppermute x3, starting transfers between devices, rotate(): lax.ppermute(block, axis, [(i, (i + distance) % n) for i in range(n)])  6.37 us
    dot_general x1, matrix products, body(): jnp.dot(others[back - 1], columns, preferred_element_type=jnp.float32)  4.86 us
  transfers between devices with their start and end apart: 6, of which 6 were waited for; matrix products, arithmetic and copies ran while one was open for 2% of the time, Pallas kernels for 1%

commit v1 on v0

--- a/solution.py
+++ b/solution.py
@@ -94,8 +94,39 @@
     tokens_ref[:, D:] = terms.astype(jnp.bfloat16)
 
 
+def stage_kernel(after_ref, *refs):
+    *refs, sems = refs
+    half = len(refs) // 2
+    copies = [
+        pltpu.make_async_copy(refs[i], refs[half + i], sems.at[i]) for i in range(half)
+    ]
+    for copy in copies:
+        copy.start()
+    for copy in copies:
+        copy.wait()
+
+
 def expert_kernel(
-    experts_all, slots, expert_ref, tokens_ref, gate_ref, up_ref, down_ref, out_ref, picked_ref
+    experts_all, slots, expert_ref, tokens_hbm, gate_ref, up_ref, down_ref, out_hbm, picked_ref
+):
+    expert = expert_ref[0]
+
+    def tile(tokens_ref, out_ref):
+        expert_tile(
+            experts_all, slots, expert, tokens_ref, gate_ref, up_ref, down_ref, out_ref, picked_ref
+        )
+
+    total, width = tokens_hbm.shape
+    pltpu.emit_pipeline(
+        tile,
+        grid=(total // TILE,),
+        in_specs=[pl.BlockSpec((TILE, width), lambda i: (i, 0))],
+        out_specs=[pl.BlockSpec((TILE, D), lambda i: (i, 0))],
+    )(tokens_hbm, out_hbm)
+
+
+def expert_tile(
+    experts_all, slots, expert, tokens_ref, gate_ref, up_ref, down_ref, out_ref, picked_ref
 ):
     groups = tokens_ref.shape[0] // GROUP
     row = lax.broadcasted_iota(jnp.int32, (GROUP, GROUP), 0)
@@ -108,7 +139,7 @@
         at = pl.ds(g * GROUP, GROUP)
         terms = tokens_ref[at, D:].astype(jnp.float32)
         column = lax.broadcasted_iota(jnp.int32, terms.shape, 1)
-        mine = (lax.rem(column, experts_all) == expert_ref[0]) & (column < TERMS * experts_all)
+        mine = (lax.rem(column, experts_all) == expert) & (column < TERMS * experts_all)
         gates = jnp.sum(jnp.where(mine, terms, 0.0), axis=1, keepdims=True)
         named = jnp.broadcast_to(gates > 0.0, (GROUP, LANES))
         rank = jnp.dot(
@@ -159,27 +190,42 @@
     )(position.reshape(1), queries, *blocks)
 
 
+def stage(after, arrays):
+    return pl.pallas_call(
+        stage_kernel,
+        out_shape=[jax.ShapeDtypeStruct(array.shape, array.dtype) for array in arrays],
+        in_specs=[pl.BlockSpec(memory_space=pl.ANY)] * (1 + len(arrays)),
+        out_specs=[vmem()] * len(arrays),
+        scratch_shapes=[pltpu.SemaphoreType.DMA((len(arrays),))],
+        compiler_params=pltpu.CompilerParams(vmem_limit_bytes=44 * 1024 * 1024),
+        cost_estimate=pl.CostEstimate(
+            flops=0,
+            bytes_accessed=2 * sum(array.size * array.dtype.itemsize for array in arrays),
+            transcendentals=0,
+        ),
+        name="stage",
+    )(after, *arrays)
+
+
 def run_expert(experts_all, block_rows, expert, tokens, w_gate, w_up, w_down):
-    total, width = tokens.shape
+    total = tokens.shape[0]
     ef = w_gate.shape[1]
     share = block_rows * TOP // experts_all
     capacity = min(block_rows, share + block_rows * TOP // (16 * experts_all))
     slots = min(GROUP, -(-(GROUP // block_rows * capacity) // 16) * 16)
-    held = pl.Buffered(1)
     return pl.pallas_call(
         functools.partial(expert_kernel, experts_all, slots),
-        grid=(total // TILE,),
         out_shape=jax.ShapeDtypeStruct((total, D), jnp.bfloat16),
         in_specs=[
             smem(),
-            pl.BlockSpec((TILE, width), lambda i: (i, 0)),
-            pl.BlockSpec((D, ef), lambda i: (0, 0), pipeline_mode=held),
-            pl.BlockSpec((D, ef), lambda i: (0, 0), pipeline_mode=held),
-            pl.BlockSpec((ef, D), lambda i: (0, 0), pipeline_mode=held),
+            pl.BlockSpec(memory_space=pl.ANY),
+            vmem(),
+            vmem(),
+            vmem(),
         ],
-        out_specs=pl.BlockSpec((TILE, D), lambda i: (i, 0)),
+        out_specs=pl.BlockSpec(memory_space=pl.ANY),
         scratch_shapes=[pltpu.VMEM((TILE // GROUP * slots, D), jnp.bfloat16)],
-        compiler_params=pltpu.CompilerParams(vmem_limit_bytes=36 * 1024 * 1024),
+        compiler_params=pltpu.CompilerParams(vmem_limit_bytes=44 * 1024 * 1024),
         cost_estimate=pl.CostEstimate(
             flops=4 * total * D * ef, bytes_accessed=4 * total * D + 6 * D * ef, transcendentals=0
         ),
@@ -235,9 +281,10 @@
     tokens_all = lax.all_gather(tokens, "exp", axis=0, tiled=True, axis_index_groups=ring)
     partial = None
     for local in range(local_experts):
+        weights = stage(tokens, (w_gate[local], w_up[local], w_down[local]))
         expert = lax.axis_index("exp") * local_experts + local
         weighted = run_expert(
-            experts_all, rows, expert, tokens_all, w_gate[local], w_up[local], w_down[local]
+            experts_all, rows, expert, tokens_all, *weights
         )
         partial = weighted if partial is None else partial + weighted
     expert_sum = lax.psum_scatter(

time: 223 us -> 221 us (level)
  waiting for transfers between devices: 157 us -> 148 us
  Pallas kernels: 22.3 us -> 27.4 us
    all_gather x1, waiting for transfers between devices: 52.1 us -> 43.4 us  [body(): lax.all_gather(tokens, 'exp', axis=0, tiled=True, axis_index_groups=ring)]
    pallas_call x1 -> x2, Pallas kernels: 19 us -> 24.1 us  [the longest x1 20.3 us: run_expert(): pl.pallas_call(functools.partial(expert_kernel, experts_all, slots), out_...]
    unnamed x20 -> x24, local copies, waits for them, and re-layouts: 13.8 us -> 15.5 us
  transfers between devices with their start and end apart: 6 -> 6, of which waited for: 6 -> 6; matrix products, arithmetic and copies ran while one was open for 2% -> 2% of each run, Pallas kernels for 1% -> 3%
where the time goes in v1:
time: 221 us; the launch traced here: 220 us
  waiting for transfers between devices  148 us (67%)
  Pallas kernels  27.4 us (12%)
  local copies, waits for them, and re-layouts  17 us (8%)
  between operations  13.2 us (6%)
  starting transfers between devices  6.46 us (3%)
  matrix products  6.19 us (3%)
    reduce_scatter x1, waiting for transfers between devices, body(): lax.psum_scatter(partial, 'exp', scatter_dimension=0, axis_index_groups=r...  57.4 us
    all_gather x1, waiting for transfers between devices, body(): lax.all_gather(tokens, 'exp', axis=0, tiled=True, axis_index_groups=ring)  43.4 us
    ppermute x3, waiting for transfers between devices, rotate(): lax.ppermute(block, axis, [(i, (i + distance) % n) for i in range(n)])  29.7 us
    pallas_call x1, Pallas kernels, run_expert(): pl.pallas_call(functools.partial(expert_kernel, experts_all, slots), out_...  20.3 us
    all_gather x1, waiting for transfers between devices, body(): lax.all_gather(columns, 'exp', axis=0, tiled=True, axis_index_groups=ring)  17.3 us
    unnamed x24, local copies, waits for them, and re-layouts  15.5 us
    ppermute x3, starting transfers between devices, rotate(): lax.ppermute(block, axis, [(i, (i + distance) % n) for i in range(n)])  6.37 us
    dot_general x1, matrix products, body(): jnp.dot(others[back - 1], columns, preferred_element_type=jnp.float32)  4.86 us
  transfers between devices with their start and end apart: 6, of which 6 were waited for; matrix products, arithmetic and copies ran while one was open for 2% of the time, Pallas kernels for 3%

profile of v1, /device:TPU:0, one launch (start us, length us, event | category | flops | bytes accessed | tf_op | source)
XLA Modules:
  0.0 220.1 jit_solution(3247313434991719808)
XLA Ops:
  6.5 0.0 copy-start
  6.5 0.0 all-gather.3.cloned.1.call-start
  6.5 1.2 copy-done
  7.8 0.8 constant_dynamic-slice_fusion
  8.6 0.0 all-gather.3.cloned.1.call-update
  8.6 0.0 all-gather.5.cloned.1.call-start
  8.7 3.0 %collective-permute-start = (bf16[128,512]{1,0:T(8,128)(2,1)}, bf16[128,512]{1,0:T(8,128)(2,1)S(1)}, u32[]{:S(2)}, u32[]{:S(2)}) collective-permute-start(bf16[128,512]{1,0:T(8,128)(2,1)} %bitcast.20), channel_id=1, source_target_pairs={{0,16},{16,0},{1,17},{17,1},{2,18},{18,2},{3,19},{19,3},{4,20},{20... | collective-permute-start | bytes 393224 | tf_op jit(solution)/shard_map/ppermute | solution.py:32
  11.7 3.7 %collective-permute-done.refs_1_ = bf16[128,512]{1,0:T(8,128)(2,1)S(1)} collective-permute-done((bf16[128,512]{1,0:T(8,128)(2,1)}, bf16[128,512]{1,0:T(8,128)(2,1)S(1)}, u32[]{:S(2)}, u32[]{:S(2)}) %collective-permute-start) | collective-permute-done | bytes 131104 | tf_op jit(solution)/shard_map/ppermute | solution.py:32
  15.4 0.0 copy-start.1
  15.4 1.2 copy-done.1
  16.6 0.0 copy-start.3
  16.6 0.9 copy-done.3
  17.5 2.0 attention.1
  19.5 1.8 collective-permute-start.1
  21.3 0.7 reshape.11.refs_2_
  22.0 0.8 copy.11
  22.8 0.8 copy.12
  23.6 20.3 %collective-permute-done.1 = bf16[128,4096]{1,0:T(8,128)(2,1)S(1)} collective-permute-done((bf16[128,4096]{1,0:T(8,128)(2,1)S(1)}, bf16[128,4096]{1,0:T(8,128)(2,1)S(1)}, u32[]{:S(2)}, u32[]{:S(2)}) %collective-permute-start.1) | collective-permute-done | bytes 1048608 | tf_op jit(solution)/shard_map/ppermute | solution.py:32
  44.0 17.3 %all-gather.3.cloned.1.call-done = bf16[4096,1024]{1,0:T(8,128)(2,1)} async-done(((bf16[256,1024]{1,0:T(8,128)(2,1)}), bf16[4096,1024]{1,0:T(8,128)(2,1)}) %all-gather.3.cloned.1.call-update) | async-done | bytes 8388624 | tf_op jit(solution)/shard_map/all_gather | solution.py:248
  61.3 0.0 copy-start.10
  61.3 4.9 %convolution_convert_fusion = bf16[128,1024]{1,0:T(8,128)(2,1)S(1)} fusion(bf16[128,4096]{1,0:T(8,128)(2,1)S(1)} %collective-permute-done.1, bf16[4096,1024]{1,0:T(8,128)(2,1)} %all-gather.3.cloned.1.call-done), kind=kOutput, calls=%fused_computation | convolution fusion | flops 1073872896 | bytes 9699328 | tf_op jit(solution)/shard_map/dot_general | solution.py:255
  66.1 0.0 copy-start.2
  66.2 1.5 collective-permute-start.2
  67.7 0.0 copy-done.10
  67.7 1.3 fusion.1.refs_0_
  69.0 5.6 %collective-permute-done.2.refs_1_ = bf16[128,1024]{1,0:T(8,128)(2,1)S(1)} collective-permute-done((bf16[128,1024]{1,0:T(8,128)(2,1)S(1)}, bf16[128,1024]{1,0:T(8,128)(2,1)S(1)}, u32[]{:S(2)}, u32[]{:S(2)}) %collective-permute-start.2) | collective-permute-done | bytes 262176 | tf_op jit(solution)/shard_map/ppermute | solution.py:32
  74.7 0.0 copy-done.2
  74.7 1.4 norm.1
  76.0 0.0 all-gather.5.cloned.1.call-update
  76.1 0.0 reduce-scatter.2.cloned.1.call-start
  76.1 3.8 %stage.1 = (bf16[2048,768]{1,0:T(8,128)(2,1)S(1)}, bf16[2048,768]{1,0:T(8,128)(2,1)S(1)}, bf16[768,2048]{1,0:T(8,128)(2,1)S(1)}) custom-call(bf16[128,2176]{1,0:T(8,128)(2,1)} %get-tuple-element.11.after_ref, bf16[2048,768]{1,0:T(8,128)(2,1)} %bitcast.22, bf16[2048,768]{1,0:T(8,128)(2,1)} %bitcast.23, bf16[768,2048]{1,0:T(8,128)(2,1)} %bitcast.24), custom_call_target="tpu_custom_call" | custom-call | bytes 18874368 | tf_op jit(solution)/shard_map/stage/pallas_call | solution.py:194
  79.9 0.0 copy-start.4
  79.9 1.6 copy-done.4
  81.5 0.0 copy-start.6
  81.5 1.7 copy-done.6
  83.2 0.0 copy-start.8
  83.2 1.6 copy-done.8
  84.8 43.4 %all-gather.5.cloned.1.call-done.tokens_hbm = bf16[2048,2176]{1,0:T(8,128)(2,1)} async-done(((bf16[128,2176]{1,0:T(8,128)(2,1)}), bf16[2048,2176]{1,0:T(8,128)(2,1)}) %all-gather.5.cloned.1.call-update) | async-done | bytes 8912912 | tf_op jit(solution)/shard_map/all_gather | solution.py:281
  128.3 0.0 copy-start.5
  128.3 1.9 copy-done.5
  130.1 0.0 copy-start.7
  130.2 1.9 copy-done.7
  132.0 0.0 copy-start.9
  132.0 1.9 copy-done.9
  133.9 20.3 %experts.1 = bf16[2048,2048]{1,0:T(8,128)(2,1)} custom-call(s32[1]{0:T(128)} %bitcast.6.expert_ref, bf16[2048,2176]{1,0:T(8,128)(2,1)} %all-gather.5.cloned.1.call-done.tokens_hbm, bf16[2048,768]{1,0:T(8,128)(2,1)S(1)} %copy-done.5, bf16[2048,768]{1,0:T(8,128)(2,1)S(1)} %copy-done.7, bf16[768,2048]{1,0:T(8,128)(2,1)S(1)} %copy-done.9), custom_call_target="tpu_custom_call" | custom-call | flops 12884901888 | bytes 26214400 | tf_op jit(solution)/shard_map/experts/pallas_call | solution.py:216
  154.2 0.0 reduce-scatter.2.cloned.1.call-update
  154.2 57.4 %reduce-scatter.2.cloned.1.call-done = bf16[128,2048]{1,0:T(8,128)(2,1)} async-done(((bf16[2048,2048]{1,0:T(8,128)(2,1)}), bf16[128,2048]{1,0:T(8,128)(2,1)}) %reduce-scatter.2.cloned.1.call-update) | async-done | bytes 524304 | tf_op jit(solution)/shard_map/reduce_scatter | solution.py:290
  211.6 1.9 fusion
Async XLA Ops:
  6.5 1.2 copy-start
  6.5 54.7 %all-gather.3.cloned.1.call-start = ((), (), s32[]{:S(2)}) async-start(), calls=%async_computation.1 | async-start | bytes 8912896 | tf_op jit(solution)/shard_map/all_gather | solution.py:248
  8.6 119.6 %all-gather.5.cloned.1.call-start = ((), (), s32[]{:S(2)}) async-start(), calls=%async_computation.2 | async-start | bytes 9469952 | tf_op jit(solution)/shard_map/all_gather | solution.py:281
  8.7 6.7 %collective-permute-start = (bf16[128,512]{1,0:T(8,128)(2,1)}, bf16[128,512]{1,0:T(8,128)(2,1)S(1)}, u32[]{:S(2)}, u32[]{:S(2)}) collective-permute-start(bf16[128,512]{1,0:T(8,128)(2,1)} %bitcast.20), channel_id=1, source_target_pairs={{0,16},{16,0},{1,17},{17,1},{2,18},{18,2},{3,19},{19,3},{4,20},{20... | collective-permute-start | bytes 393224 | tf_op jit(solution)/shard_map/ppermute | solution.py:32
  15.4 1.2 copy-start.1
  16.6 0.9 copy-start.3
  19.5 24.4 %collective-permute-start.1 = (bf16[128,4096]{1,0:T(8,128)(2,1)S(1)}, bf16[128,4096]{1,0:T(8,128)(2,1)S(1)}, u32[]{:S(2)}, u32[]{:S(2)}) collective-permute-start(bf16[128,4096]{1,0:T(8,128)(2,1)S(1)} %attention.1), channel_id=1, source_target_pairs={{0,16},{16,0},{1,17},{17,1},{2,18},{18,2},{3,19},{19,3},{4,20},{20... | collective-permute-start | bytes 3145736 | tf_op jit(solution)/shard_map/ppermute | solution.py:32
  61.3 6.4 %copy-start.10 = (bf16[4096,1024]{1,0:T(8,128)(2,1)S(1)}, bf16[4096,1024]{1,0:T(8,128)(2,1)}, u32[]{:S(2)}) copy-start(bf16[4096,1024]{1,0:T(8,128)(2,1)} %all-gather.3.cloned.1.call-done) | copy-start | bytes 25165828
  66.1 8.5 %copy-start.2 = (bf16[1,128,2048]{2,1,0:T(8,128)(2,1)S(1)}, bf16[1,128,2048]{2,1,0:T(8,128)(2,1)}, u32[]{:S(2)}) copy-start(bf16[1,128,2048]{2,1,0:T(8,128)(2,1)} %param.10) | copy-start | bytes 1572868
  66.2 8.5 %collective-permute-start.2 = (bf16[128,1024]{1,0:T(8,128)(2,1)S(1)}, bf16[128,1024]{1,0:T(8,128)(2,1)S(1)}, u32[]{:S(2)}, u32[]{:S(2)}) collective-permute-start(bf16[128,1024]{1,0:T(8,128)(2,1)S(1)} %convolution_convert_fusion), channel_id=1, source_target_pairs={{0,16},{16,0},{1,17},{17,1},{2,18},{18,2},{3,19},{19,3},{4,20},{20... | collective-permute-start | bytes 786440 | tf_op jit(solution)/shard_map/ppermute | solution.py:32
  76.1 135.5 %reduce-scatter.2.cloned.1.call-start = ((), (), s32[]{:S(2)}) async-start(), calls=%async_computation.3 | async-start | bytes 8912896 | tf_op jit(solution)/shard_map/reduce_scatter | solution.py:290
  79.9 1.6 copy-start.4
  81.5 1.7 copy-start.6
  83.2 1.6 copy-start.8
  128.3 1.9 copy-start.5
  130.1 1.9 copy-start.7
  132.0 1.9 copy-start.9
Sparse Core Ops, SparseCore 0:
  9.0 52.2 all-gather.2
  76.2 52.0 all-gather.4
  154.4 57.1 reduce-scatter.1

commit v2 on v0

--- a/solution.py
+++ b/solution.py
@@ -14,8 +14,9 @@
 TOP = 8
 LANES = 128
 TERMS = 3
-TILE = 512
 GROUP = 256
+BATCHES = 2
+PIECES = 2
 
 
 def chip_ring(n):
@@ -95,44 +96,118 @@
 
 
 def expert_kernel(
-    experts_all, slots, expert_ref, tokens_ref, gate_ref, up_ref, down_ref, out_ref, picked_ref
+    experts_all,
+    slots,
+    expert_ref,
+    tokens_hbm,
+    gate_hbm,
+    up_hbm,
+    down_hbm,
+    out_hbm,
+    tokens_ref,
+    gate_ref,
+    up_ref,
+    down_ref,
+    picked_ref,
+    weights_ref,
+    places_ref,
+    in_sems,
+    weight_sems,
+    out_sems,
 ):
-    groups = tokens_ref.shape[0] // GROUP
+    groups = tokens_ref.shape[0]
+    batch = groups // BATCHES
+
+    def tokens_in(g):
+        at = pl.ds(pl.multiple_of(g * GROUP, GROUP), GROUP)
+        return pltpu.make_async_copy(tokens_hbm.at[at], tokens_ref.at[g], in_sems.at[g])
+
+    def result_out(g):
+        at = pl.ds(pl.multiple_of(g * GROUP, GROUP), GROUP)
+        return pltpu.make_async_copy(
+            tokens_ref.at[g, :, pl.ds(0, D)], out_hbm.at[at], out_sems.at[g]
+        )
+
+    def weight_in(number, source, target):
+        rows = source.shape[0] // PIECES
+        return [
+            pltpu.make_async_copy(
+                source.at[pl.ds(i * rows, rows)],
+                target.at[pl.ds(i * rows, rows)],
+                weight_sems.at[number * PIECES + i],
+            )
+            for i in range(PIECES)
+        ]
+
+    gate_in = weight_in(0, gate_hbm, gate_ref)
+    up_in = weight_in(1, up_hbm, up_ref)
+    down_in = weight_in(2, down_hbm, down_ref)
+    for g in range(batch):
+        tokens_in(g).start()
+    for copy in gate_in + up_in + down_in:
+        copy.start()
+    for g in range(batch, groups):
+        tokens_in(g).start()
+
     row = lax.broadcasted_iota(jnp.int32, (GROUP, GROUP), 0)
     col = lax.broadcasted_iota(jnp.int32, (GROUP, GROUP), 1)
     up_to = (row >= col).astype(jnp.bfloat16)
     slot_row = lax.broadcasted_iota(jnp.int32, (slots, GROUP), 0).astype(jnp.float32)
     slot_col = lax.broadcasted_iota(jnp.int32, (GROUP, slots), 1).astype(jnp.float32)
-    weights, places = [], []
+
+    def wait_first(number, copies):
+        @pl.when(number == 0)
+        def _():
+            for copy in copies:
+                copy.wait()
+
+    def run_batch(number, carry):
+        def pick(i, carry):
+            g = number * batch + i
+            tokens_in(g).wait()
+            terms = tokens_ref[g, :, D:].astype(jnp.float32)
+            column = lax.broadcasted_iota(jnp.int32, terms.shape, 1)
+            mine = lax.rem(column, experts_all) == expert_ref[0]
+            mine = mine & (column < TERMS * experts_all)
+            gates = jnp.sum(jnp.where(mine, terms, 0.0), axis=1, keepdims=True)
+            gates = jnp.broadcast_to(gates, (GROUP, LANES))
+            named = gates > 0.0
+            rank = jnp.dot(up_to, named.astype(jnp.bfloat16), preferred_element_type=jnp.float32)
+            place = jnp.where(named, rank - 1.0, -1.0)
+            chosen = (slot_row == jnp.transpose(place)[:1]).astype(jnp.bfloat16)
+            picked = jnp.dot(chosen, tokens_ref[g, :, :D], preferred_element_type=jnp.float32)
+            at = pl.ds(pl.multiple_of(i * slots, slots), slots)
+            picked_ref[at, :] = picked.astype(jnp.bfloat16)
+            weights_ref[i] = gates
+            places_ref[i] = place
+            return carry
+
+        lax.fori_loop(0, batch, pick, 0)
+        wait_first(number, gate_in)
+        gate_pre = jnp.dot(picked_ref[...], gate_ref[...], preferred_element_type=jnp.float32)
+        wait_first(number, up_in)
+        up_pre = jnp.dot(picked_ref[...], up_ref[...], preferred_element_type=jnp.float32)
+        activated = (gate_pre / (1.0 + jnp.exp(-gate_pre)) * up_pre).astype(jnp.bfloat16)
+        wait_first(number, down_in)
+        picked_ref[...] = jnp.dot(
+            activated, down_ref[...], preferred_element_type=jnp.float32
+        ).astype(jnp.bfloat16)
+
+        def put(i, carry):
+            g = number * batch + i
+            at = pl.ds(pl.multiple_of(i * slots, slots), slots)
+            spread = (slot_col == places_ref[i][:, :1]).astype(jnp.bfloat16)
+            expert_out = jnp.dot(spread, picked_ref[at, :], preferred_element_type=jnp.float32)
+            tokens_ref[g, :, :D] = (expert_out * weights_ref[i][:, :1]).astype(jnp.bfloat16)
+            result_out(g).start()
+            return carry
+
+        lax.fori_loop(0, batch, put, 0)
+        return carry
+
+    lax.fori_loop(0, BATCHES, run_batch, 0)
     for g in range(groups):
-        at = pl.ds(g * GROUP, GROUP)
-        terms = tokens_ref[at, D:].astype(jnp.float32)
-        column = lax.broadcasted_iota(jnp.int32, terms.shape, 1)
-        mine = (lax.rem(column, experts_all) == expert_ref[0]) & (column < TERMS * experts_all)
-        gates = jnp.sum(jnp.where(mine, terms, 0.0), axis=1, keepdims=True)
-        named = jnp.broadcast_to(gates > 0.0, (GROUP, LANES))
-        rank = jnp.dot(
-            up_to, named.astype(jnp.bfloat16), preferred_element_type=jnp.float32
-        )
-        place = jnp.where(named, rank - 1.0, -1.0)
-        pick = (slot_row == jnp.transpose(place)[:1]).astype(jnp.bfloat16)
-        picked = jnp.dot(pick, tokens_ref[at, :D], preferred_element_type=jnp.float32)
-        picked_ref[pl.ds(g * slots, slots), :] = picked.astype(jnp.bfloat16)
-        weights.append(gates)
-        places.append(place[:, :1])
-    picked = picked_ref[...]
-    gate_pre = jnp.dot(picked, gate_ref[...], preferred_element_type=jnp.float32)
-    up_pre = jnp.dot(picked, up_ref[...], preferred_element_type=jnp.float32)
-    activated = (gate_pre / (1.0 + jnp.exp(-gate_pre)) * up_pre).astype(jnp.bfloat16)
-    picked_ref[...] = jnp.dot(
-        activated, down_ref[...], preferred_element_type=jnp.float32
-    ).astype(jnp.bfloat16)
-    for g in range(groups):
-        put = (slot_col == places[g]).astype(jnp.bfloat16)
-        expert_out = jnp.dot(
-            put, picked_ref[pl.ds(g * slots, slots), :], preferred_element_type=jnp.float32
-        )
-        out_ref[pl.ds(g * GROUP, GROUP), :] = (expert_out * weights[g]).astype(jnp.bfloat16)
+        result_out(g).wait()
 
 
 def vmem():
@@ -165,21 +240,27 @@
     share = block_rows * TOP // experts_all
     capacity = min(block_rows, share + block_rows * TOP // (16 * experts_all))
     slots = min(GROUP, -(-(GROUP // block_rows * capacity) // 16) * 16)
-    held = pl.Buffered(1)
+    groups = total // GROUP
+    batch = groups // BATCHES
+    anywhere = pl.BlockSpec(memory_space=pl.ANY)
     return pl.pallas_call(
         functools.partial(expert_kernel, experts_all, slots),
-        grid=(total // TILE,),
         out_shape=jax.ShapeDtypeStruct((total, D), jnp.bfloat16),
-        in_specs=[
-            smem(),
-            pl.BlockSpec((TILE, width), lambda i: (i, 0)),
-            pl.BlockSpec((D, ef), lambda i: (0, 0), pipeline_mode=held),
-            pl.BlockSpec((D, ef), lambda i: (0, 0), pipeline_mode=held),
-            pl.BlockSpec((ef, D), lambda i: (0, 0), pipeline_mode=held),
+        in_specs=[smem()] + [anywhere] * 4,
+        out_specs=anywhere,
+        scratch_shapes=[
+            pltpu.VMEM((groups, GROUP, width), jnp.bfloat16),
+            pltpu.VMEM((D, ef), jnp.bfloat16),
+            pltpu.VMEM((D, ef), jnp.bfloat16),
+            pltpu.VMEM((ef, D), jnp.bfloat16),
+            pltpu.VMEM((batch * slots, D), jnp.bfloat16),
+            pltpu.VMEM((batch, GROUP, LANES), jnp.float32),
+            pltpu.VMEM((batch, GROUP, LANES), jnp.float32),
+            pltpu.SemaphoreType.DMA((groups,)),
+            pltpu.SemaphoreType.DMA((3 * PIECES,)),
+            pltpu.SemaphoreType.DMA((groups,)),
         ],
-        out_specs=pl.BlockSpec((TILE, D), lambda i: (i, 0)),
-        scratch_shapes=[pltpu.VMEM((TILE // GROUP * slots, D), jnp.bfloat16)],
-        compiler_params=pltpu.CompilerParams(vmem_limit_bytes=36 * 1024 * 1024),
+        compiler_params=pltpu.CompilerParams(vmem_limit_bytes=56 * 1024 * 1024),
         cost_estimate=pl.CostEstimate(
             flops=4 * total * D * ef, bytes_accessed=4 * total * D + 6 * D * ef, transcendentals=0
         ),

time: 223 us -> 220 us (0.987)
  local copies, waits for them, and re-layouts: 15.4 us -> 6.47 us
  Pallas kernels: 22.3 us -> 29.2 us
    unnamed x20 -> x12, local copies, waits for them, and re-layouts: 13.8 us -> 4.93 us
    pallas_call x1, Pallas kernels: 19 us -> 25.9 us  [run_expert(): pl.pallas_call(functools.partial(expert_kernel, experts_all, slots), out_...]
where the time goes in v2:
time: 220 us
  waiting for transfers between devices  157 us (71%)
  Pallas kernels  29.2 us (13%)
  between operations  13.2 us (6%)
  local copies, waits for them, and re-layouts  6.47 us (3%)
  starting transfers between devices  6.46 us (3%)
  matrix products  6.19 us (3%)
    reduce_scatter x1, waiting for transfers between devices, body(): lax.psum_scatter(partial, 'exp', scatter_dimension=0, axis_index_groups=r...  57.4 us
    all_gather x1, waiting for transfers between devices, body(): lax.all_gather(tokens, 'exp', axis=0, tiled=True, axis_index_groups=ring)  52.1 us
    ppermute x3, waiting for transfers between devices, rotate(): lax.ppermute(block, axis, [(i, (i + distance) % n) for i in range(n)])  29.7 us
    pallas_call x1, Pallas kernels, run_expert(): pl.pallas_call(functools.partial(expert_kernel, experts_all, slots), out_...  25.9 us
    all_gather x1, waiting for transfers between devices, body(): lax.all_gather(columns, 'exp', axis=0, tiled=True, axis_index_groups=ring)  17.3 us
    ppermute x3, starting transfers between devices, rotate(): lax.ppermute(block, axis, [(i, (i + distance) % n) for i in range(n)])  6.37 us
    unnamed x12, local copies, waits for them, and re-layouts  4.93 us
    dot_general x1, matrix products, body(): jnp.dot(others[back - 1], columns, preferred_element_type=jnp.float32)  4.86 us
  transfers between devices with their start and end apart: 6, of which 6 were waited for; matrix products, arithmetic and copies ran while one was open for 2% of the time, Pallas kernels for 1%

profile of v2, /device:TPU:0, one launch (start us, length us, event | category | flops | bytes accessed | tf_op | source)
XLA Modules:
  0.0 220.0 jit_solution(16299043658979826037)
XLA Ops:
  6.5 0.0 copy-start
  6.5 0.0 all-gather.3.cloned.1.call-start
  6.5 1.2 copy-done
  7.8 0.8 constant_dynamic-slice_fusion
  8.6 0.0 all-gather.3.cloned.1.call-update
  8.6 0.0 all-gather.5.cloned.1.call-start
  8.7 3.0 %collective-permute-start = (bf16[128,512]{1,0:T(8,128)(2,1)}, bf16[128,512]{1,0:T(8,128)(2,1)S(1)}, u32[]{:S(2)}, u32[]{:S(2)}) collective-permute-start(bf16[128,512]{1,0:T(8,128)(2,1)} %bitcast.20), channel_id=1, source_target_pairs={{0,16},{16,0},{1,17},{17,1},{2,18},{18,2},{3,19},{19,3},{4,20},{20... | collective-permute-start | bytes 393224 | tf_op jit(solution)/shard_map/ppermute | solution.py:33
  11.7 3.7 %collective-permute-done.refs_1_ = bf16[128,512]{1,0:T(8,128)(2,1)S(1)} collective-permute-done((bf16[128,512]{1,0:T(8,128)(2,1)}, bf16[128,512]{1,0:T(8,128)(2,1)S(1)}, u32[]{:S(2)}, u32[]{:S(2)}) %collective-permute-start) | collective-permute-done | bytes 131104 | tf_op jit(solution)/shard_map/ppermute | solution.py:33
  15.4 0.0 copy-start.1
  15.4 1.2 copy-done.1
  16.6 0.0 copy-start.3
  16.6 0.9 copy-done.3
  17.5 2.0 attention.1
  19.5 1.8 collective-permute-start.1
  21.3 0.7 reshape.11.refs_2_
  22.0 0.8 copy.11
  22.8 0.8 copy.12
  23.6 20.3 %collective-permute-done.1 = bf16[128,4096]{1,0:T(8,128)(2,1)S(1)} collective-permute-done((bf16[128,4096]{1,0:T(8,128)(2,1)S(1)}, bf16[128,4096]{1,0:T(8,128)(2,1)S(1)}, u32[]{:S(2)}, u32[]{:S(2)}) %collective-permute-start.1) | collective-permute-done | bytes 1048608 | tf_op jit(solution)/shard_map/ppermute | solution.py:33
  44.0 17.3 %all-gather.3.cloned.1.call-done = bf16[4096,1024]{1,0:T(8,128)(2,1)} async-done(((bf16[256,1024]{1,0:T(8,128)(2,1)}), bf16[4096,1024]{1,0:T(8,128)(2,1)}) %all-gather.3.cloned.1.call-update) | async-done | bytes 8388624 | tf_op jit(solution)/shard_map/all_gather | solution.py:283
  61.3 0.0 copy-start.4
  61.3 4.9 %convolution_convert_fusion = bf16[128,1024]{1,0:T(8,128)(2,1)S(1)} fusion(bf16[128,4096]{1,0:T(8,128)(2,1)S(1)} %collective-permute-done.1, bf16[4096,1024]{1,0:T(8,128)(2,1)} %all-gather.3.cloned.1.call-done), kind=kOutput, calls=%fused_computation | convolution fusion | flops 1073872896 | bytes 9699328 | tf_op jit(solution)/shard_map/dot_general | solution.py:290
  66.1 0.0 copy-start.2
  66.2 1.5 collective-permute-start.2
  67.7 0.0 copy-done.4
  67.7 1.3 fusion.1.refs_0_
  69.0 5.6 %collective-permute-done.2.refs_1_ = bf16[128,1024]{1,0:T(8,128)(2,1)S(1)} collective-permute-done((bf16[128,1024]{1,0:T(8,128)(2,1)S(1)}, bf16[128,1024]{1,0:T(8,128)(2,1)S(1)}, u32[]{:S(2)}, u32[]{:S(2)}) %collective-permute-start.2) | collective-permute-done | bytes 262176 | tf_op jit(solution)/shard_map/ppermute | solution.py:33
  74.7 0.0 copy-done.2
  74.7 1.4 norm.1
  76.1 0.0 all-gather.5.cloned.1.call-update
  76.1 0.0 reduce-scatter.2.cloned.1.call-start
  76.1 52.1 %all-gather.5.cloned.1.call-done.tokens_hbm = bf16[2048,2176]{1,0:T(8,128)(2,1)} async-done(((bf16[128,2176]{1,0:T(8,128)(2,1)}), bf16[2048,2176]{1,0:T(8,128)(2,1)}) %all-gather.5.cloned.1.call-update) | async-done | bytes 8912912 | tf_op jit(solution)/shard_map/all_gather | solution.py:316
  128.3 25.9 %experts.1 = bf16[2048,2048]{1,0:T(8,128)(2,1)} custom-call(s32[1]{0:T(128)} %bitcast.6.expert_ref, bf16[2048,2176]{1,0:T(8,128)(2,1)} %all-gather.5.cloned.1.call-done.tokens_hbm, bf16[2048,768]{1,0:T(8,128)(2,1)} %bitcast.22, bf16[2048,768]{1,0:T(8,128)(2,1)} %bitcast.23, bf16[768,2048]{1,0:T(8,128)(2,1)} %bitcast.24), custom_call_target="tpu_custom_call" | custom-call | flops 12884901888 | bytes 26214400 | tf_op jit(solution)/shard_map/experts/pallas_call | solution.py:246
  154.2 0.0 reduce-scatter.2.cloned.1.call-update
  154.2 57.4 %reduce-scatter.2.cloned.1.call-done = bf16[128,2048]{1,0:T(8,128)(2,1)} async-done(((bf16[2048,2048]{1,0:T(8,128)(2,1)}), bf16[128,2048]{1,0:T(8,128)(2,1)}) %reduce-scatter.2.cloned.1.call-update) | async-done | bytes 524304 | tf_op jit(solution)/shard_map/reduce_scatter | solution.py:324
  211.5 1.9 fusion
Async XLA Ops:
  6.5 1.2 copy-start
  6.5 54.7 %all-gather.3.cloned.1.call-start = ((), (), s32[]{:S(2)}) async-start(), calls=%async_computation.1 | async-start | bytes 8912896 | tf_op jit(solution)/shard_map/all_gather | solution.py:283
  8.6 119.7 %all-gather.5.cloned.1.call-start = ((), (), s32[]{:S(2)}) async-start(), calls=%async_computation.2 | async-start | bytes 9469952 | tf_op jit(solution)/shard_map/all_gather | solution.py:316
  8.7 6.7 %collective-permute-start = (bf16[128,512]{1,0:T(8,128)(2,1)}, bf16[128,512]{1,0:T(8,128)(2,1)S(1)}, u32[]{:S(2)}, u32[]{:S(2)}) collective-permute-start(bf16[128,512]{1,0:T(8,128)(2,1)} %bitcast.20), channel_id=1, source_target_pairs={{0,16},{16,0},{1,17},{17,1},{2,18},{18,2},{3,19},{19,3},{4,20},{20... | collective-permute-start | bytes 393224 | tf_op jit(solution)/shard_map/ppermute | solution.py:33
  15.4 1.2 copy-start.1
  16.6 0.9 copy-start.3
  19.5 24.4 %collective-permute-start.1 = (bf16[128,4096]{1,0:T(8,128)(2,1)S(1)}, bf16[128,4096]{1,0:T(8,128)(2,1)S(1)}, u32[]{:S(2)}, u32[]{:S(2)}) collective-permute-start(bf16[128,4096]{1,0:T(8,128)(2,1)S(1)} %attention.1), channel_id=1, source_target_pairs={{0,16},{16,0},{1,17},{17,1},{2,18},{18,2},{3,19},{19,3},{4,20},{20... | collective-permute-start | bytes 3145736 | tf_op jit(solution)/shard_map/ppermute | solution.py:33
  61.3 6.4 %copy-start.4 = (bf16[4096,1024]{1,0:T(8,128)(2,1)S(1)}, bf16[4096,1024]{1,0:T(8,128)(2,1)}, u32[]{:S(2)}) copy-start(bf16[4096,1024]{1,0:T(8,128)(2,1)} %all-gather.3.cloned.1.call-done) | copy-start | bytes 25165828
  66.1 8.5 %copy-start.2 = (bf16[1,128,2048]{2,1,0:T(8,128)(2,1)S(1)}, bf16[1,128,2048]{2,1,0:T(8,128)(2,1)}, u32[]{:S(2)}) copy-start(bf16[1,128,2048]{2,1,0:T(8,128)(2,1)} %param.10) | copy-start | bytes 1572868
  66.2 8.5 %collective-permute-start.2 = (bf16[128,1024]{1,0:T(8,128)(2,1)S(1)}, bf16[128,1024]{1,0:T(8,128)(2,1)S(1)}, u32[]{:S(2)}, u32[]{:S(2)}) collective-permute-start(bf16[128,1024]{1,0:T(8,128)(2,1)S(1)} %convolution_convert_fusion), channel_id=1, source_target_pairs={{0,16},{16,0},{1,17},{17,1},{2,18},{18,2},{3,19},{19,3},{4,20},{20... | collective-permute-start | bytes 786440 | tf_op jit(solution)/shard_map/ppermute | solution.py:33
  76.1 135.5 %reduce-scatter.2.cloned.1.call-start = ((), (), s32[]{:S(2)}) async-start(), calls=%async_computation.3 | async-start | bytes 8912896 | tf_op jit(solution)/shard_map/reduce_scatter | solution.py:324
Sparse Core Ops, SparseCore 0:
  9.0 52.2 all-gather.2
  76.2 52.0 all-gather.4
  154.3 57.1 reduce-scatter.1

commit v3 on v2

--- a/solution.py
+++ b/solution.py
@@ -15,7 +15,7 @@
 LANES = 128
 TERMS = 3
 GROUP = 256
-BATCHES = 2
+BATCHES = 4
 PIECES = 2
 
 
@@ -28,9 +28,28 @@
     return [2 * chip + core for chip in chip_ring(n) for core in range(2)]
 
 
+def core_rings(n):
+    return [[2 * chip + core for chip in chip_ring(n)] for core in range(2)]
+
+
+def swap_cores(block):
+    n = lax.axis_size("exp")
+    return lax.ppermute(block, "exp", [(i, i ^ 1) for i in range(n)])
+
+
 def rotate(block, axis, distance):
+    if distance == 0:
+        return block
     n = lax.axis_size(axis)
     return lax.ppermute(block, axis, [(i, (i + distance) % n) for i in range(n)])
+
+
+def columns_kernel(pos_ref, source, target, sem):
+    wide = target.shape[1]
+    at = pl.ds(pl.multiple_of(pos_ref[0] * wide, wide), wide)
+    copy = pltpu.make_async_copy(source.at[:, at], target, sem)
+    copy.start()
+    copy.wait()
 
 
 def attention_kernel(places, pos_ref, query_ref, *refs):
@@ -63,8 +82,9 @@
             mixed = jnp.dot(
                 weights.astype(jnp.bfloat16), values, preferred_element_type=jnp.float32
             )
-            at = places[head]
-            out_ref[:, at : at + HD] = (mixed / row_sum).astype(jnp.bfloat16)
+            core, at = places[head]
+            slot = lax.rem(core + pos_ref[1], 2)
+            out_ref[slot, :, at : at + HD] = (mixed / row_sum).astype(jnp.bfloat16)
 
 
 def norm_kernel(experts_all, pos_ref, hidden_ref, *refs):
@@ -144,10 +164,8 @@
     down_in = weight_in(2, down_hbm, down_ref)
     for g in range(batch):
         tokens_in(g).start()
-    for copy in gate_in + up_in + down_in:
+    for copy in gate_in:
         copy.start()
-    for g in range(batch, groups):
-        tokens_in(g).start()
 
     row = lax.broadcasted_iota(jnp.int32, (GROUP, GROUP), 0)
     col = lax.broadcasted_iota(jnp.int32, (GROUP, GROUP), 1)
@@ -155,11 +173,13 @@
     slot_row = lax.broadcasted_iota(jnp.int32, (slots, GROUP), 0).astype(jnp.float32)
     slot_col = lax.broadcasted_iota(jnp.int32, (GROUP, slots), 1).astype(jnp.float32)
 
-    def wait_first(number, copies):
+    def at_first(number, arrived, following):
         @pl.when(number == 0)
         def _():
-            for copy in copies:
+            for copy in arrived:
                 copy.wait()
+            for copy in following:
+                copy.start()
 
     def run_batch(number, carry):
         def pick(i, carry):
@@ -183,12 +203,13 @@
             return carry
 
         lax.fori_loop(0, batch, pick, 0)
-        wait_first(number, gate_in)
+        at_first(number, [], up_in)
+        at_first(number, gate_in, down_in)
         gate_pre = jnp.dot(picked_ref[...], gate_ref[...], preferred_element_type=jnp.float32)
-        wait_first(number, up_in)
+        at_first(number, up_in, [tokens_in(g) for g in range(batch, 2 * batch)])
         up_pre = jnp.dot(picked_ref[...], up_ref[...], preferred_element_type=jnp.float32)
         activated = (gate_pre / (1.0 + jnp.exp(-gate_pre)) * up_pre).astype(jnp.bfloat16)
-        wait_first(number, down_in)
+        at_first(number, down_in, [tokens_in(g) for g in range(2 * batch, groups)])
         picked_ref[...] = jnp.dot(
             activated, down_ref[...], preferred_element_type=jnp.float32
         ).astype(jnp.bfloat16)
@@ -218,20 +239,34 @@
     return pl.BlockSpec(memory_space=pltpu.SMEM)
 
 
-def attend(position, queries, blocks, n_exp, proj_rows):
-    ring = device_ring(n_exp)
+def own_columns(position, matrix, n_parts):
+    rows, width = matrix.shape
+    return pl.pallas_call(
+        columns_kernel,
+        out_shape=jax.ShapeDtypeStruct((rows, width // n_parts), matrix.dtype),
+        in_specs=[smem(), pl.BlockSpec(memory_space=pl.ANY)],
+        out_specs=pl.BlockSpec(memory_space=pl.ANY),
+        scratch_shapes=[pltpu.SemaphoreType.DMA(())],
+        compiler_params=pltpu.CompilerParams(vmem_limit_bytes=60 * 1024 * 1024),
+        name="columns",
+    )(position.reshape(1), matrix)
+
+
+def attend(position, core, queries, blocks, n_exp, proj_rows):
+    rows = queries.shape[0]
+    rings = core_rings(n_exp)
     places = {}
     for head in range(QH):
         device, inside = divmod(head * HD, proj_rows)
-        places[head] = ring.index(device) * proj_rows + inside
+        places[head] = (device % 2, rings[device % 2].index(device) * proj_rows + inside)
     return pl.pallas_call(
         functools.partial(attention_kernel, places),
-        out_shape=jax.ShapeDtypeStruct(queries.shape, jnp.bfloat16),
+        out_shape=jax.ShapeDtypeStruct((2, rows, QH * HD // 2), jnp.bfloat16),
         in_specs=[smem()] + [vmem()] * (1 + len(blocks)),
         out_specs=vmem(),
         compiler_params=pltpu.CompilerParams(vmem_limit_bytes=16 * 1024 * 1024),
         name="attention",
-    )(position.reshape(1), queries, *blocks)
+    )(jnp.stack([position, core]), queries, *blocks)
 
 
 def run_expert(experts_all, block_rows, expert, tokens, w_gate, w_up, w_down):
@@ -278,18 +313,30 @@
     proj_rows = out_proj.shape[0]
     ring = [device_ring(n_exp)]
 
-    wide = D // n_ctx
-    columns = lax.dynamic_slice_in_dim(out_proj, position * wide, wide, axis=1)
-    columns = lax.all_gather(columns, "exp", axis=0, tiled=True, axis_index_groups=ring)
-
+    columns = lax.all_gather(
+        own_columns(position, out_proj, n_ctx),
+        "exp",
+        axis=0,
+        tiled=True,
+        axis_index_groups=core_rings(n_exp),
+    )
+
+    def times_columns(block):
+        return jnp.dot(block, columns, preferred_element_type=jnp.float32)
+
+    core = lax.axis_index("exp") % 2
     blocks = [keyval[0]] + [rotate(keyval[0], "ctx", back) for back in range(1, n_ctx)]
-    attended = attend(position, query[0], blocks, n_exp, proj_rows)
-    others = [rotate(attended, "ctx", back) for back in range(1, n_ctx)]
+    attended = attend(position, core, query[0], blocks, n_exp, proj_rows)
+    own_heads, other_heads = attended[0], attended[1]
+    sibling_heads = swap_cores(other_heads)
     projected = []
-    for back in range(1, n_ctx):
-        part = jnp.dot(others[back - 1], columns, preferred_element_type=jnp.float32)
-        projected.append(rotate(part.astype(jnp.bfloat16), "ctx", -back))
-    projected = [jnp.dot(attended, columns, preferred_element_type=jnp.float32)] + projected
+    for back in range(n_ctx):
+        heads = [rotate(own_heads, "ctx", back), rotate(sibling_heads, "ctx", back)]
+        from_sibling = swap_cores(times_columns(heads[1]).astype(jnp.bfloat16))
+        part = times_columns(heads[0]) + from_sibling.astype(jnp.float32)
+        if back:
+            part = rotate(part.astype(jnp.bfloat16), "ctx", -back)
+        projected.append(part)
 
     local_experts = w_gate.shape[0]
     experts_all = n_exp * local_experts

time: 220 us -> 235 us (1.068)
  Pallas kernels: 29.2 us -> 48.5 us
  local copies, waits for them, and re-layouts: 6.47 us -> 2.72 us
    pallas_call x0 -> x1, Pallas kernels: none -> 17 us  [own_columns(): pl.pallas_call(columns_kernel, out_shape=jax.ShapeDtypeStruct((rows, widt...]
    ppermute x3 -> x4, waiting for transfers between devices: 29.7 us -> 22.2 us  [rotate(): lax.ppermute(block, axis, [(i, (i + distance) % n) for i in range(n)])]
    all_gather x1, waiting for transfers between devices: 17.3 us -> 22.3 us  [body(): lax.all_gather(own_columns(position, out_proj, n_ctx), 'exp', axis=0, til...]
    unnamed x12 -> x16, local copies, waits for them, and re-layouts: 4.93 us -> 2.65 us
    dot_general x2 -> x4, matrix products: 6.19 us -> 5.33 us  [times_columns(): return jnp.dot(block, columns, preferred_element_type=jnp.float32)]
    ppermute x3 -> x4, starting transfers between devices: 6.37 us -> 6.66 us  [rotate(): lax.ppermute(block, axis, [(i, (i + distance) % n) for i in range(n)])]
  transfers between devices with their start and end apart: 6 -> 10, of which waited for: 6 -> 8; matrix products, arithmetic and copies ran while one was open for 2% -> 2% of each run, Pallas kernels for 1% -> 1%
where the time goes in v3:
time: 235 us
  waiting for transfers between devices  156 us (66%)
  Pallas kernels  48.5 us (21%)
  between operations  13.2 us (6%)
  starting transfers between devices  7.17 us (3%)
  matrix products  5.33 us (2%)
  local copies, waits for them, and re-layouts  2.72 us (1%)
    reduce_scatter x1, waiting for transfers between devices, body(): lax.psum_scatter(partial, 'exp', scatter_dimension=0, axis_index_groups=r...  57.4 us
    all_gather x1, waiting for transfers between devices, body(): lax.all_gather(tokens, 'exp', axis=0, tiled=True, axis_index_groups=ring)  52.2 us
    pallas_call x1, Pallas kernels, run_expert(): pl.pallas_call(functools.partial(expert_kernel, experts_all, slots), out_...  27.5 us
    all_gather x1, waiting for transfers between devices, body(): lax.all_gather(own_columns(position, out_proj, n_ctx), 'exp', axis=0, til...  22.3 us
    ppermute x4, waiting for transfers between devices, rotate(): lax.ppermute(block, axis, [(i, (i + distance) % n) for i in range(n)])  22.2 us
    pallas_call x1, Pallas kernels, own_columns(): pl.pallas_call(columns_kernel, out_shape=jax.ShapeDtypeStruct((rows, widt...  17 us
    ppermute x4, starting transfers between devices, rotate(): lax.ppermute(block, axis, [(i, (i + distance) % n) for i in range(n)])  6.66 us
    dot_general x4, matrix products, times_columns(): return jnp.dot(block, columns, preferred_element_type=jnp.float32)  5.33 us
  transfers between devices with their start and end apart: 10, of which 8 were waited for; matrix products, arithmetic and copies ran while one was open for 2% of the time, Pallas kernels for 1%

profile of v3, /device:TPU:0, one launch (start us, length us, event | category | flops | bytes accessed | tf_op | source)
XLA Modules:
  0.0 235.2 jit_solution(11689041716415120032)
XLA Ops:
  6.5 0.0 copy-start.4
  6.5 0.0 copy-start.5
  6.5 0.0 copy-start.6
  6.5 0.0 all-gather.3.cloned.1.call-start
  6.5 17.0 %columns.1 = bf16[256,1024]{1,0:T(8,128)(2,1)} custom-call(s32[1]{0:T(128)} %bitcast.pos_ref, bf16[256,2048]{1,0:T(8,128)(2,1)} %source.1), custom_call_target="tpu_custom_call" | custom-call | tf_op jit(solution)/shard_map/columns/pallas_call | solution.py:244
  23.5 0.0 all-gather.3.cloned.1.call-update
  23.6 0.0 all-gather.5.cloned.1.call-start
  23.6 3.0 %collective-permute-start = (bf16[128,512]{1,0:T(8,128)(2,1)}, bf16[128,512]{1,0:T(8,128)(2,1)S(1)}, u32[]{:S(2)}, u32[]{:S(2)}) collective-permute-start(bf16[128,512]{1,0:T(8,128)(2,1)} %bitcast.29), channel_id=1, source_target_pairs={{0,16},{16,0},{1,17},{17,1},{2,18},{18,2},{3,19},{19,3},{4,20},{20... | collective-permute-start | bytes 393224 | tf_op jit(solution)/shard_map/ppermute | solution.py:44
  26.6 0.1 pad_add_fusion.pos_ref
  26.7 3.6 %collective-permute-done.refs_1_ = bf16[128,512]{1,0:T(8,128)(2,1)S(1)} collective-permute-done((bf16[128,512]{1,0:T(8,128)(2,1)}, bf16[128,512]{1,0:T(8,128)(2,1)S(1)}, u32[]{:S(2)}, u32[]{:S(2)}) %collective-permute-start) | collective-permute-done | bytes 131104 | tf_op jit(solution)/shard_map/ppermute | solution.py:44
  30.4 1.2 copy-done
  31.6 0.0 copy-start.2
  31.6 0.9 copy-done.2
  32.5 2.6 %attention.1 = bf16[2,128,2048]{2,1,0:T(8,128)(2,1)S(1)} custom-call(s32[2]{0:T(128)S(1)} %pad_add_fusion.pos_ref, bf16[128,4096]{1,0:T(8,128)(2,1)S(1)} %bitcast.25, bf16[128,512]{1,0:T(8,128)(2,1)S(1)} %bitcast.30, bf16[128,512]{1,0:T(8,128)(2,1)S(1)} %collective-permute-done.refs_1_), custom_call_target="tpu_custom_call" | custom-call | tf_op jit(solution)/shard_map/attention/pallas_call | solution.py:262
  35.2 0.1 slice_bitcast_fusion.1
  35.2 0.1 collective-permute-start.1
  35.3 1.9 collective-permute-done.1
  37.2 1.7 collective-permute-start.4
  38.9 0.0 copy-done.4
  38.9 0.0 copy-done.5
  39.0 0.1 copy.11
  39.1 0.0 copy-done.6
  39.1 0.1 copy.12
  39.2 0.4 collective-permute-start.3
  39.5 12.5 %collective-permute-done.4 = bf16[128,2048]{1,0:T(8,128)(2,1)S(1)} collective-permute-done((bf16[128,2048]{1,0:T(8,128)(2,1)S(1)}, bf16[128,2048]{1,0:T(8,128)(2,1)S(1)}, u32[]{:S(2)}, u32[]{:S(2)}) %collective-permute-start.4) | collective-permute-done | bytes 524320 | tf_op jit(solution)/shard_map/ppermute | solution.py:44
  52.0 22.3 %all-gather.3.cloned.1.call-done = bf16[2048,1024]{1,0:T(8,128)(2,1)} async-done(((bf16[256,1024]{1,0:T(8,128)(2,1)}), bf16[2048,1024]{1,0:T(8,128)(2,1)}) %all-gather.3.cloned.1.call-update) | async-done | bytes 4194320 | tf_op jit(solution)/shard_map/all_gather | solution.py:316
  74.3 3.1 %convolution_convert_fusion = bf16[128,1024]{1,0:T(8,128)(2,1)S(1)} fusion(bf16[128,2048]{1,0:T(8,128)(2,1)S(1)} %collective-permute-done.4, bf16[2048,1024]{1,0:T(8,128)(2,1)} %all-gather.3.cloned.1.call-done), kind=kOutput, calls=%fused_computation.3 | convolution fusion | flops 537001984 | bytes 4980736 | tf_op jit(solution)/shard_map/dot_general | solution.py:325
  77.4 0.1 collective-permute-start.5
  77.5 0.3 copy-done.3
  77.8 0.7 convolution_convert_fusion.1
  78.5 0.0 copy-start.1
  78.5 0.3 collective-permute-start.2
  78.8 0.0 collective-permute-done.3
  78.8 0.2 collective-permute-done.5
  79.0 0.7 fusion
  79.8 1.5 collective-permute-start.6
  81.3 0.0 collective-permute-done.2
  81.3 0.8 convolution_add_fusion.1.refs_0_
  82.1 6.1 %collective-permute-done.6.refs_1_ = bf16[128,1024]{1,0:T(8,128)(2,1)S(1)} collective-permute-done((bf16[128,1024]{1,0:T(8,128)(2,1)S(1)}, bf16[128,1024]{1,0:T(8,128)(2,1)S(1)}, u32[]{:S(2)}, u32[]{:S(2)}) %collective-permute-start.6) | collective-permute-done | bytes 262176 | tf_op jit(solution)/shard_map/ppermute | solution.py:44
  88.2 0.0 copy-done.1
  88.2 1.4 norm.1
  89.6 0.0 all-gather.5.cloned.1.call-update
  89.6 0.0 reduce-scatter.2.cloned.1.call-start
  89.6 52.2 %all-gather.5.cloned.1.call-done.tokens_hbm = bf16[2048,2176]{1,0:T(8,128)(2,1)} async-done(((bf16[128,2176]{1,0:T(8,128)(2,1)}), bf16[2048,2176]{1,0:T(8,128)(2,1)}) %all-gather.5.cloned.1.call-update) | async-done | bytes 8912912 | tf_op jit(solution)/shard_map/all_gather | solution.py:363
  141.8 27.5 %experts.1 = bf16[2048,2048]{1,0:T(8,128)(2,1)} custom-call(s32[1]{0:T(128)} %bitcast.9.expert_ref, bf16[2048,2176]{1,0:T(8,128)(2,1)} %all-gather.5.cloned.1.call-done.tokens_hbm, bf16[2048,768]{1,0:T(8,128)(2,1)} %bitcast.31, bf16[2048,768]{1,0:T(8,128)(2,1)} %bitcast.32, bf16[768,2048]{1,0:T(8,128)(2,1)} %bitcast.33), custom_call_target="tpu_custom_call" | custom-call | flops 12884901888 | bytes 26214400 | tf_op jit(solution)/shard_map/experts/pallas_call | solution.py:281
  169.3 0.0 reduce-scatter.2.cloned.1.call-update
  169.3 57.4 %reduce-scatter.2.cloned.1.call-done = bf16[128,2048]{1,0:T(8,128)(2,1)} async-done(((bf16[2048,2048]{1,0:T(8,128)(2,1)}), bf16[128,2048]{1,0:T(8,128)(2,1)}) %reduce-scatter.2.cloned.1.call-update) | async-done | bytes 524304 | tf_op jit(solution)/shard_map/reduce_scatter | solution.py:371
  226.8 1.9 fusion.1
  (3 shorter events, 0.0 us)
Async XLA Ops:
  6.5 32.4 %copy-start.4 = (bf16[2048]{0:T(1024)(128)(2,1)S(1)}, bf16[2048]{0:T(1024)(128)(2,1)}, u32[]{:S(2)}) copy-start(bf16[2048]{0:T(1024)(128)(2,1)} %param.14) | copy-start | bytes 12292
  6.5 32.4 %copy-start.5 = (s32[1,128,8]{1,2,0:T(8,128)S(1)}, s32[1,128,8]{1,2,0:T(8,128)}, u32[]{:S(2)}) copy-start(s32[1,128,8]{1,2,0:T(8,128)} %param.15) | copy-start | bytes 12292
  6.5 32.5 %copy-start.6 = (f32[1,128,8]{1,2,0:T(8,128)S(1)}, f32[1,128,8]{1,2,0:T(8,128)}, u32[]{:S(2)}) copy-start(f32[1,128,8]{1,2,0:T(8,128)} %param.16) | copy-start | bytes 12292
  6.5 67.8 %all-gather.3.cloned.1.call-start = ((), (), s32[]{:S(2)}) async-start(), calls=%async_computation.1 | async-start | bytes 4718592 | tf_op jit(solution)/shard_map/all_gather | solution.py:316
  23.6 118.2 %all-gather.5.cloned.1.call-start = ((), (), s32[]{:S(2)}) async-start(), calls=%async_computation.2 | async-start | bytes 9469952 | tf_op jit(solution)/shard_map/all_gather | solution.py:363
  23.6 6.7 %collective-permute-start = (bf16[128,512]{1,0:T(8,128)(2,1)}, bf16[128,512]{1,0:T(8,128)(2,1)S(1)}, u32[]{:S(2)}, u32[]{:S(2)}) collective-permute-start(bf16[128,512]{1,0:T(8,128)(2,1)} %bitcast.29), channel_id=1, source_target_pairs={{0,16},{16,0},{1,17},{17,1},{2,18},{18,2},{3,19},{19,3},{4,20},{20... | collective-permute-start | bytes 393224 | tf_op jit(solution)/shard_map/ppermute | solution.py:44
  30.4 1.2 copy-start
  31.6 0.9 copy-start.2
  35.2 2.0 collective-permute-start.1
  37.2 14.8 %collective-permute-start.4 = (bf16[128,2048]{1,0:T(8,128)(2,1)S(1)}, bf16[128,2048]{1,0:T(8,128)(2,1)S(1)}, u32[]{:S(2)}, u32[]{:S(2)}) collective-permute-start(bf16[128,2048]{1,0:T(8,128)(2,1)S(1)} %collective-permute-done.1), channel_id=1, source_target_pairs={{0,16},{16,0},{1,17},{17,1},{2,18},{18,2},{3,19},{19,3},{4,20},{20... | collective-permute-start | bytes 1572872 | tf_op jit(solution)/shard_map/ppermute | solution.py:44
  39.2 39.7 %collective-permute-start.3 = (bf16[128,2048]{1,0:T(8,128)(2,1)S(1)}, bf16[128,2048]{1,0:T(8,128)(2,1)S(1)}, u32[]{:S(2)}, u32[]{:S(2)}) collective-permute-start(bf16[128,2048]{1,0:T(8,128)(2,1)S(1)} %get-tuple-element.9), channel_id=1, source_target_pairs={{0,16},{16,0},{1,17},{17,1},{2,18},{18,2},{3,19},{19,3},{4,20},{20... | collective-permute-start | bytes 1572872 | tf_op jit(solution)/shard_map/ppermute | solution.py:44
  74.3 3.4 %copy-start.3 = (bf16[2048,1024]{1,0:T(8,128)(2,1)S(1)}, bf16[2048,1024]{1,0:T(8,128)(2,1)}, u32[]{:S(2)}) copy-start(bf16[2048,1024]{1,0:T(8,128)(2,1)} %all-gather.3.cloned.1.call-done) | copy-start | bytes 12582916
  77.4 1.6 collective-permute-start.5
  78.5 9.7 %copy-start.1 = (bf16[1,128,2048]{2,1,0:T(8,128)(2,1)S(1)}, bf16[1,128,2048]{2,1,0:T(8,128)(2,1)}, u32[]{:S(2)}) copy-start(bf16[1,128,2048]{2,1,0:T(8,128)(2,1)} %param.10) | copy-start | bytes 1572868
  78.5 2.8 %collective-permute-start.2 = (bf16[128,1024]{1,0:T(8,128)(2,1)S(1)}, bf16[128,1024]{1,0:T(8,128)(2,1)S(1)}, u32[]{:S(2)}, u32[]{:S(2)}) collective-permute-start(bf16[128,1024]{1,0:T(8,128)(2,1)S(1)} %convolution_convert_fusion.1), channel_id=1, source_target_pairs={{0,1},{1,0},{2,3},{3,2},{4,5},{5,4},{6,7},{7,6},{8,9},{9,8},{10,11... | collective-permute-start | bytes 786440 | tf_op jit(solution)/shard_map/ppermute | solution.py:37
  79.8 8.4 %collective-permute-start.6 = (bf16[128,1024]{1,0:T(8,128)(2,1)S(1)}, bf16[128,1024]{1,0:T(8,128)(2,1)S(1)}, u32[]{:S(2)}, u32[]{:S(2)}) collective-permute-start(bf16[128,1024]{1,0:T(8,128)(2,1)S(1)} %fusion), channel_id=1, source_target_pairs={{0,16},{16,0},{1,17},{17,1},{2,18},{18,2},{3,19},{19,3},{4,20},{20... | collective-permute-start | bytes 786440 | tf_op jit(solution)/shard_map/ppermute | solution.py:44
  89.6 137.2 %reduce-scatter.2.cloned.1.call-start = ((), (), s32[]{:S(2)}) async-start(), calls=%async_computation.3 | async-start | bytes 8912896 | tf_op jit(solution)/shard_map/reduce_scatter | solution.py:371
Sparse Core Ops, SparseCore 0:
  23.7 50.5 all-gather.2
  89.7 52.0 all-gather.4
  169.5 57.2 reduce-scatter.1
